TPU v7x, 32 devices: a whole 2x2x4 slice. The times are simulated.
32 devices in a mesh: sec: 4 (over z), row: 4 (over x, core), col: 2 (over y).
Axes of the slice: x: 2, y: 2, z: 4, core: 2. Of those that a mesh axis runs over, the one named last changes fastest.
Arguments:
- amps: bfloat16 [16, 32, 32, 512], P(None, ('sec', 'row'), 'col'), may hold values from -6 to 6
- driver: bfloat16 [16, 32, 32, 512], P(None, 'col', ('sec', 'row')), may hold values from -6 to 6
- ladder_operator: bfloat16 [16384, 16384], P('col', ('sec', 'row')), as said below
- ladder_block_mask: int32 [128, 128], P('col', ('sec', 'row')), may hold values from 0 to 1, as said below
- cycle_op: bfloat16 [16384, 16384], P(('sec', 'row'), 'col'), as said below
- cycle_mask: int32 [128, 128], P(('sec', 'row'), 'col'), may hold values from 0 to 1, as said below
- occ_i: float32 [16], replicated, may hold values from -2 to -0.3
- occ_j: float32 [32], replicated, may hold values from -2 to -0.3
- vir_a: float32 [32], replicated, may hold values from 0.2 to 3
- vir_b: float32 [512], replicated, may hold values from 0.2 to 3
Outputs:
- amp_one: float32 [16, 32, 32, 512], P(None, 'col', ('sec', 'row'))
- amp_two: float32 [16, 32, 32, 512], P(None, ('sec', 'row'), 'col')
Inputs may be any that keep to these rules, and one draw needn't show every extreme that they name: ladder_operator is symmetric. cycle_op is symmetric. ladder_block_mask is symmetric with ones on its diagonal. cycle_mask is symmetric with ones on its diagonal.
All inputs are finite; a program needn't handle non-finite values.
Results may differ from a plain program's by a relative error of at most 0.0024.
Values may be sent and summed in bfloat16 or wider, within the bound.
A program may use at most 192 MiB of HBM per device.

v0:
```python
import jax
import jax.numpy as jnp
from jax import lax
from jax.sharding import PartitionSpec as P


def tile_masked(tile, mask):
    rows_blocks = mask.shape[0]
    cols_blocks = mask.shape[1]
    row_edge = tile.shape[0] // rows_blocks
    col_edge = tile.shape[1] // cols_blocks
    shaped = tile.reshape(rows_blocks, row_edge, cols_blocks, col_edge)
    return (shaped * mask[:, None, :, None].astype(tile.dtype)).reshape(tile.shape)


def product_transposed(rows, tile):
    return lax.dot_general(rows, tile, (((1,), (1,)), ((), ())), preferred_element_type=jnp.float32)


def denominator(occ_i, occ_part, vir_part, vir_b):
    return (
        vir_part[None, None, :, None]
        + vir_b[None, None, None, :]
        - occ_i[:, None, None, None]
        - occ_part[None, :, None, None]
    )


def body(
    amps,
    driver,
    ladder_operator,
    ladder_block_mask,
    cycle_op,
    cycle_mask,
    occ_i,
    occ_j,
    vir_a,
    vir_b,
):
    wide_count = lax.axis_size(("sec", "row"))
    col_count = lax.axis_size("col")
    wide_index = lax.axis_index(("sec", "row"))
    col_index = lax.axis_index("col")
    occupied = amps.shape[0]
    virtuals = amps.shape[3]
    occ_all = occ_j.shape[0]
    vir_all = vir_a.shape[0]
    occ_wide = occ_all // wide_count
    occ_cols = occ_all // col_count
    vir_wide = vir_all // wide_count
    vir_cols = vir_all // col_count
    ladder_tile = tile_masked(ladder_operator, ladder_block_mask)
    cycle_tile = tile_masked(cycle_op, cycle_mask)
    piece = lax.all_gather(amps, ("sec", "row"), axis=1, tiled=True)
    count = piece.shape[1]
    rows = piece.reshape(occupied * count, vir_cols * virtuals)
    result = jnp.dot(rows, ladder_tile, preferred_element_type=jnp.float32)
    ladder_part = result.reshape(occupied, count, vir_wide, virtuals)
    ladder_one = lax.psum_scatter(ladder_part, "col", scatter_dimension=1, tiled=True)
    base = driver.astype(jnp.float32) + ladder_one
    piece = lax.all_gather(amps, "col", axis=2, tiled=True)
    count = piece.shape[2]
    rows = jnp.transpose(piece, (0, 2, 1, 3)).reshape(occupied * count, occ_wide * virtuals)
    result = jnp.dot(rows, cycle_tile, preferred_element_type=jnp.float32)
    cycle_part = result.reshape(occupied, count, occ_cols, virtuals)
    cycle_one = lax.psum_scatter(cycle_part, ("sec", "row"), scatter_dimension=1, tiled=True)
    occ_here = lax.dynamic_slice_in_dim(occ_j, col_index * occ_cols, occ_cols)
    combined = base + jnp.transpose(cycle_one, (0, 2, 1, 3))
    vir_here = lax.dynamic_slice_in_dim(vir_a, wide_index * vir_wide, vir_wide)
    amp_one = combined / denominator(occ_i, occ_here, vir_here, vir_b)
    amp_rounded = amp_one.astype(jnp.bfloat16)
    piece = lax.all_gather(amp_rounded, ("sec", "row"), axis=2, tiled=True)
    count = piece.shape[2]
    rows = jnp.transpose(piece, (0, 2, 1, 3)).reshape(occupied * count, occ_cols * virtuals)
    result = product_transposed(rows, cycle_tile)
    cycle_part_two = result.reshape(occupied, count, occ_wide, virtuals)
    piece = lax.all_gather(amp_rounded, "col", axis=1, tiled=True)
    count = piece.shape[1]
    rows = piece.reshape(occupied * count, vir_wide * virtuals)
    result = product_transposed(rows, ladder_tile)
    ladder_part_two = result.reshape(occupied, count, vir_cols, virtuals)
    ladder_two = lax.psum_scatter(ladder_part_two, ("sec", "row"), scatter_dimension=1, tiled=True)
    cycle_two = lax.psum_scatter(cycle_part_two, "col", scatter_dimension=1, tiled=True)
    occ_mine = lax.dynamic_slice_in_dim(occ_j, wide_index * occ_wide, occ_wide)
    vir_mine = lax.dynamic_slice_in_dim(vir_a, col_index * vir_cols, vir_cols)
    total_two = ladder_two + jnp.transpose(cycle_two, (0, 2, 1, 3))
    amp_two = total_two / denominator(occ_i, occ_mine, vir_mine, vir_b)
    return (amp_one, amp_two)


def solution(mesh):
    placed = (
        P(None, ("sec", "row"), "col", None),
        P(None, "col", ("sec", "row"), None),
        P("col", ("sec", "row")),
        P("col", ("sec", "row")),
        P(("sec", "row"), "col"),
        P(("sec", "row"), "col"),
        P(),
        P(),
        P(),
        P(),
    )
    return jax.shard_map(
        body,
        mesh=mesh,
        in_specs=placed,
        out_specs=(P(None, "col", ("sec", "row"), None), P(None, ("sec", "row"), "col", None)),
        check_vma=False,
    )
```

profile of v0, /device:TPU:15, one launch (start us, length us, event | category | flops | bytes accessed | tf_op | source)
XLA Modules:
  0.0 753.1 jit_solution(8255286820509054223)
XLA Ops:
  7.2 0.7 all-gather.5.cloned.1.call-update
  7.9 0.7 all-gather.7.cloned.1.call-update
  8.7 0.7 convert_element_type.16
  9.4 0.7 convert_element_type.15
  10.1 0.1 copy.43
  10.2 2.8 mul.33
  13.0 2.9 copy-done
  16.0 6.1 bitcast_multiply_fusion.1
  22.1 63.0 %all-gather.5.cloned.1.call-done = bf16[16,32,16,512]{3,2,1,0:T(8,128)(2,1)} async-done(((bf16[16,2,16,512]{3,2,1,0:T(8,128)(2,1)}), bf16[16,32,16,512]{3,2,1,0:T(8,128)(2,1)}) %all-gather.5.cloned.1.call-update) | async-done | bytes 8388624 | tf_op jit(solution)/shard_map/all_gather | solution.py:55
  85.1 16.4 %copy.64 = bf16[64,8,16,512]{3,1,2,0:T(8,128)(2,1)} copy(bf16[64,8,16,512]{3,2,1,0:T(8,128)(2,1)} %bitcast.58) | data formatting | bytes 16777216
  101.5 16.1 %convolution_bitcast_fusion.1 = f32[512,1024]{0,1:T(8,128)} fusion(bf16[8192,1024]{1,0:T(8,128)(2,1)} %bitcast_multiply_fusion.1, bf16[512,8192]{1,0:T(8,128)(2,1)} %bitcast.61), kind=kOutput, calls=%fused_computation.5 | convolution fusion | flops 8589934592 | bytes 27262976 | tf_op jit(solution)/shard_map/dot_general | solution.py:58
  117.7 1.9 copy.44
  119.6 2.8 reshape.115
  122.4 4.2 copy.45
  126.6 5.0 mul.36
  131.7 14.3 %bitcast_multiply_fusion = bf16[1024,8192]{1,0:T(8,128)(2,1)} fusion(bf16[1024,8192]{1,0:T(8,128)(2,1)} %param.14, bf16[128,8,64,128]{3,2,1,0:T(8,128)(2,1)S(1)} %bitcast.53), kind=kLoop, calls=%fused_computation | loop fusion | flops 8388608 | bytes 50331648 | tf_op jit(solution)/shard_map/mul | solution.py:13
  146.0 2.3 copy.46
  148.3 0.2 copy.66
  148.5 15.9 %convolution_bitcast_fusion = f32[512,8192]{0,1:T(8,128)} fusion(bf16[1024,8192]{1,0:T(8,128)(2,1)} %bitcast_multiply_fusion, bf16[512,1024]{1,0:T(8,128)(2,1)S(1)} %bitcast.64), kind=kOutput, calls=%fused_computation.2 | convolution fusion | flops 8589934592 | bytes 34603008 | tf_op jit(solution)/shard_map/dot_general | solution.py:65
  164.5 17.4 %copy.47 = f32[512,8192]{1,0:T(8,128)} copy(f32[512,8192]{0,1:T(8,128)} %convolution_bitcast_fusion) | data formatting | bytes 33554432 | tf_op jit(solution)/shard_map/dot_general | solution.py:65
  181.9 19.0 %copy.67 = f32[64,8,16,512]{3,2,1,0:T(8,128)S(1)} copy(f32[64,8,16,512]{3,1,2,0:T(8,128)} %bitcast.54) | data formatting | bytes 33554432
  200.9 6.3 copy.48
  207.2 0.0 all-gather.9.cloned.1.call-start
  207.2 0.5 copy-done.5
  207.8 0.1 dynamic_slice.12
  207.9 0.1 dynamic_slice.13
  207.9 0.1 broadcast_add_fusion.1
  208.0 0.1 broadcast_subtract_fusion.1
  208.1 175.5 %reduce-scatter.7.cloned.1.call-done = f32[16,2,16,512]{3,2,0,1:T(8,128)} async-done(((f32[16,32,16,512]{3,2,0,1:T(8,128)}), f32[16,2,16,512]{3,2,0,1:T(8,128)}) %reduce-scatter.7.cloned.1.call-update) | async-done | bytes 1048592 | tf_op jit(solution)/shard_map/reduce_scatter | solution.py:67
  383.6 3.6 fusion.6
  387.2 2.1 copy.52
  389.4 18.8 %all-gather.9.cloned.1.call-done = bf16[16,32,2,512]{3,0,2,1:T(8,128)(2,1)} async-done(((bf16[16,16,2,512]{3,0,2,1:T(8,128)(2,1)}), bf16[16,32,2,512]{3,0,2,1:T(8,128)(2,1)}) %all-gather.9.cloned.1.call-update) | async-done | bytes 1048592 | tf_op jit(solution)/shard_map/all_gather | solution.py:78
  408.3 2.3 copy.50
  410.6 1.7 reshape.118
  412.3 73.6 %all-gather.11.cloned.1.call-done = bf16[16,16,32,512]{3,1,0,2:T(8,128)(2,1)} async-done(((bf16[16,16,2,512]{3,1,0,2:T(8,128)(2,1)}), bf16[16,16,32,512]{3,1,0,2:T(8,128)(2,1)}) %all-gather.11.cloned.1.call-update) | async-done | bytes 8388624 | tf_op jit(solution)/shard_map/all_gather | solution.py:73
  485.9 13.4 %reshape.123 = bf16[16,32,8192]{2,0,1:T(8,128)(2,1)} reshape(bf16[16,32,16,512]{3,2,0,1:T(8,128)(2,1)} %bitcast.59) | data formatting | bytes 16777216 | tf_op jit(solution)/shard_map/dot_general | solution.py:17
  499.3 28.3 %fusion = f32[16,32,2,512]{3,1,2,0:T(8,128)S(1)} fusion(bf16[2,512,8192,1]{2,1,0,3:T(8,128)(2,1)} %bitcast.57, bf16[16,32,8192,1]{2,0,1,3:T(8,128)(2,1)} %bitcast.60), kind=kOutput, calls=%fused_computation.3 | convolution fusion | flops 8589934592 | bytes 27262976 | tf_op jit(solution)/shard_map/dot_general | solution.py:17
  527.6 2.5 copy.54
  530.2 16.3 %fusion.3 = f32[16,32,16,512]{3,1,2,0:T(8,128)} fusion(bf16[16,512,1024,1]{2,1,0,3:T(8,128)(2,1)} %bitcast.56, bf16[16,32,1024,1]{2,1,0,3:T(8,128)(2,1)} %reshape.118), kind=kOutput, calls=%fused_computation.8 | convolution fusion | flops 8589934592 | bytes 34603008 | tf_op jit(solution)/shard_map/dot_general | solution.py:17
  546.5 17.7 %copy.51 = f32[16,32,16,512]{3,2,0,1:T(8,128)} copy(f32[16,32,16,512]{3,1,2,0:T(8,128)} %fusion.3) | data formatting | bytes 33554432 | tf_op jit(solution)/shard_map/dot_general | solution.py:17
  564.2 0.1 dynamic_slice.15
  564.3 0.1 dynamic_slice.14
  564.4 0.1 broadcast_add_fusion
  564.5 0.1 broadcast_subtract_fusion
  564.6 1.8 copy.56
  566.4 176.2 %reduce-scatter.9.cloned.1.call-done = f32[16,2,16,512]{3,2,0,1:T(8,128)} async-done(((f32[16,32,16,512]{3,2,0,1:T(8,128)}), f32[16,2,16,512]{3,2,0,1:T(8,128)}) %reduce-scatter.9.cloned.1.call-update) | async-done | bytes 1048592 | tf_op jit(solution)/shard_map/reduce_scatter | solution.py:83
  742.6 2.3 fusion.2
  744.9 1.1 copy.57
  (26 shorter events, 0.4 us)
Async XLA Ops:
  7.2 78.0 %all-gather.5.cloned.1.call-start = ((), (), s32[]{:S(2)}) async-start(), calls=%async_computation.4 | async-start | bytes 8912896 | tf_op jit(solution)/shard_map/all_gather | solution.py:55
  7.9 138.1 %all-gather.7.cloned.1.call-start = ((), (), s32[]{:S(2)}) async-start(), calls=%async_computation.6 | async-start | bytes 1572864 | tf_op jit(solution)/shard_map/all_gather | solution.py:62
  8.6 199.4 %reduce-scatter.5.cloned.1.call-start = ((), (), s32[]{:S(2)}) async-start(), calls=%async_computation.5 | async-start | bytes 3145728 | tf_op jit(solution)/shard_map/reduce_scatter | solution.py:60
  10.2 5.8 copy-start
  126.6 257.0 %reduce-scatter.7.cloned.1.call-start = ((), (), s32[]{:S(2)}) async-start(), calls=%async_computation.7 | async-start | bytes 17825792 | tf_op jit(solution)/shard_map/reduce_scatter | solution.py:67
  207.1 0.7 copy-start.5
  207.1 0.7 copy-start.4
  207.1 0.8 copy-start.2
  207.1 0.9 copy-start.3
  207.1 176.4 %copy-start.1 = (bf16[16,16,2,512]{3,2,1,0:T(2,128)(2,1)S(1)}, bf16[16,16,2,512]{3,2,1,0:T(2,128)(2,1)}, u32[]{:S(2)}) copy-start(bf16[16,16,2,512]{3,2,1,0:T(2,128)(2,1)} %param.11) | copy-start | bytes 1572868
  207.2 201.1 %all-gather.9.cloned.1.call-start = ((), (), s32[]{:S(2)}) async-start(), calls=%async_computation.8 | async-start | bytes 1572864 | tf_op jit(solution)/shard_map/all_gather | solution.py:78
  387.2 98.7 %all-gather.11.cloned.1.call-start = ((), (), s32[]{:S(2)}) async-start(), calls=%async_computation.10 | async-start | bytes 8912896 | tf_op jit(solution)/shard_map/all_gather | solution.py:73
  389.4 177.0 %reduce-scatter.11.cloned.1.call-start = ((), (), s32[]{:S(2)}) async-start(), calls=%async_computation.11 | async-start | bytes 3145728 | tf_op jit(solution)/shard_map/reduce_scatter | solution.py:84
  530.1 212.5 %reduce-scatter.9.cloned.1.call-start = ((), (), s32[]{:S(2)}) async-start(), calls=%async_computation.9 | async-start | bytes 17825792 | tf_op jit(solution)/shard_map/reduce_scatter | solution.py:83
Sparse Core Ops, SparseCore 0:
  10.2 74.9 all-gather.4
  86.7 19.7 all-gather.6
  126.7 30.2 reduce-scatter.4
  207.3 176.2 reduce-scatter.6
  387.3 20.9 all-gather.8
  411.1 74.7 all-gather.10
  530.3 30.2 reduce-scatter.10
  564.7 177.9 reduce-scatter.8
where the time goes:
time: 766 us; the launch traced here: 753 us
  waiting for transfers between devices  509 us (66%)
  local copies, waits for them, and re-layouts  125 us (16%)
  matrix products  76.7 us (10%)
  other arithmetic  28 us (4%)
  between operations  14.5 us (2%)
    reduce_scatter x1, waiting for transfers between devices, body(): lax.psum_scatter(ladder_part_two, ('sec', 'row'), scatter_dimension=1, ti...  176 us
    reduce_scatter x1, waiting for transfers between devices, body(): lax.psum_scatter(cycle_part, ('sec', 'row'), scatter_dimension=1, tiled=T...  175 us
    all_gather x1, waiting for transfers between devices, body(): piece = lax.all_gather(amp_rounded, ('sec', 'row'), axis=2, tiled=True)  73.6 us
    all_gather x1, waiting for transfers between devices, body(): piece = lax.all_gather(amps, ('sec', 'row'), axis=1, tiled=True)  63 us
    dot_general x2, matrix products, product_transposed(): lax.dot_general(rows, tile, (((1,), (1,)), ((), ())), preferred_element_t...  44.6 us
    unnamed x17, local copies, waits for them, and re-layouts  42 us
    dot_general x4, local copies, waits for them, and re-layouts, product_transposed(): lax.dot_general(rows, tile, (((1,), (1,)), ((), ())), preferred_element_t...  35.4 us
    mul x2, other arithmetic, tile_masked(): shaped * mask[:, None, :, None].astype(tile.dtype)  20.4 us
  transfers between devices with their start and end apart: 8, of which 5 were waited for; matrix products, arithmetic and copies ran while one was open for 23% of the time, Pallas kernels for 0%

commit v1 on v0

v1 whole, which is shorter than its diff:
```python
import functools

import jax
import jax.numpy as jnp
from jax import lax
from jax.experimental import pallas as pl
from jax.experimental.pallas import tpu as pltpu
from jax.sharding import PartitionSpec as P

MESH = pl.DeviceIdType.MESH


def kernel(
    sizes, x, drv, v_hbm, w_hbm, mv, mw, base, shift_one, shift_two, out_one, out_two,
    va, wa, xa, xb, acca, accb, sa, sb, ra, rb,
    tile_sem, own_sem, ring_s, ring_r, sib_s, sib_r, y_s, y_r, yb_s, yb_r,
    ea_s, ea_r, eb_s, eb_r, ready,
):
    S, R, C = sizes
    W = S * R
    G = W // C
    nch = W // 2
    wide, tall, occ, vir = xa.shape[1:]
    half = tall // 2
    rows = accb.shape[0]
    edge = v_hbm.shape[0] // (mv.shape[0] * mv.shape[1])
    z, row, q = lax.axis_index("sec"), lax.axis_index("row"), lax.axis_index("col")
    me = z * R + row
    core = row % 2
    xchip = row // 2
    p = xchip * S + z + (xchip % 2) * (S - 1 - 2 * z)
    sibling = (z, row + 1 - 2 * core, q)
    home = me // G

    def place(o):
        xo, zo = o // S, o % S
        return xo, zo + (xo % 2) * (S - 1 - 2 * zo)

    def wide_of(o):
        xo, zo = place(o)
        return zo * R + 2 * xo + core

    def device_at(o):
        xo, zo = place(o)
        return (zo, 2 * xo + core, q)

    after, before = device_at((p + 1) % nch), device_at((p + nch - 1) % nch)

    def origin(t, h):
        return (p + nch - t) % nch if h == 0 else (p + t) % nch

    def part(h):
        return pl.ds(h * half, half)

    def remote(src, dst, s, r, device):
        return pltpu.make_async_remote_copy(
            src_ref=src, dst_ref=dst, send_sem=s, recv_sem=r, device_id=device, device_id_type=MESH
        )

    def ring(t, h):
        piece = xa.at[wide_of(origin(t, h)), :, part(h)]
        return remote(piece, piece, ring_s.at[h, t], ring_r.at[h, t], after if h == 0 else before)

    def sib(t, h):
        piece = xa.at[wide_of(origin(t, h)), :, part(h)]
        return remote(piece, piece, sib_s.at[h, t], sib_r.at[h, t], sibling)

    def cross(t, h):
        w = wide_of(origin(t, h))
        goal = w // G
        slot = (q - goal - 1 + C) % C
        return goal, remote(
            xa.at[w, :, part(h)], xb.at[slot, w - goal * G, :, part(h)],
            y_s.at[h, t], y_r.at[slot, h, t], (z, row, goal),
        )

    def cross_in(t, h, slot):
        w = wide_of(origin(t, h))
        piece = xb.at[slot, w - (w // G) * G, :, part(h)]
        return w // G, piece

    barrier = pltpu.get_barrier_semaphore()

    def greet(d, carry):
        w, c = d // C, d % C

        @pl.when(d != me * C + q)
        def _():
            pl.semaphore_signal(barrier, inc=1, device_id=(w // R, w % R, c), device_id_type=MESH)

        return carry

    lax.fori_loop(0, W * C, greet, 0)
    own = pltpu.make_async_copy(x, xa.at[me], own_sem)
    own.start()

    def v_tile(s):
        size = va.shape[1]
        return pltpu.make_async_copy(v_hbm.at[pl.ds(s * size, size), :], va.at[s], tile_sem.at[0, s])

    def w_tile(s):
        size = wa.shape[2]
        return pltpu.make_async_copy(
            w_hbm.at[:, pl.ds(pl.multiple_of(s * size, size), size)], wa.at[s], tile_sem.at[1, s]
        )

    def load(s, carry):
        v_tile(s).start()
        w_tile(s).start()
        return carry

    own.wait()
    pl.semaphore_wait(barrier, W * C - 1)

    def masked(tile, mask, s):
        strips = mask.shape[1]
        for b in range(strips):
            span = pl.ds(b * edge, edge)
            keep = jnp.broadcast_to(mask[s, pl.ds(b, 1), :], (edge, tile.shape[2])).astype(tile.dtype)
            tile[s, span, :] = tile[s, span, :] * keep

    def product(lhs, tile, s, transposed):
        dims = (((1,), (1 if transposed else 0,)), ((), ()))
        return lax.dot_general(lhs, tile[s], dims, preferred_element_type=jnp.float32)

    def gather(sweep):
        def slot_step(t, carry):
            for h in range(2):
                @pl.when(t >= 1)
                def _():
                    ring(t - 1, h).wait_recv()

                @pl.when(t < nch - 1)
                def _():
                    ring(t, h).start()

                sib(t, h).start()
                goal, copy = cross(t, h)

                @pl.when(goal != q)
                def _():
                    copy.start()

            return carry

        lax.fori_loop(0, nch, slot_step, 0)

        def landed(t, carry):
            for h in range(2):
                sib(t, h).wait_recv()
            return carry

        lax.fori_loop(0, nch, landed, 0)

    def pass_on(t):
        for h in range(2):
            for slot in range(C - 1):
                mine, piece = cross_in(t, h, slot)

                @pl.when(mine == q)
                def _():
                    remote(piece, piece, y_s.at[h, t], y_r.at[slot, h, t], sibling).wait_recv()
                    remote(piece, piece, yb_s.at[slot, h, t], yb_r.at[slot, h, t], sibling).start()

    def settle(t, carry):
        for h in range(2):
            for slot in range(C - 1):
                mine, piece = cross_in(t, h, slot)

                @pl.when(mine == q)
                def _():
                    remote(piece, piece, yb_s.at[slot, h, t], yb_r.at[slot, h, t], sibling).wait()

            @pl.when(t < nch - 1)
            def _():
                ring(t, h).wait_send()

            sib(t, h).wait_send()
            goal, copy = cross(t, h)

            @pl.when(goal != q)
            def _():
                copy.wait_send()

        return carry

    def exchange_a(sweep, k):
        return remote(
            sa.at[k - 1], ra.at[sweep, C - 1 - k], ea_s.at[k - 1], ea_r.at[sweep, C - 1 - k], (z, row, (q + k) % C)
        )

    def exchange_b(sweep, k):
        w = (me + k) % W
        block = ((w // G - q + C) % C) * G + w % G
        return w, block, remote(
            sb.at[block], rb.at[sweep, q, me - home * G], eb_s.at[k], eb_r.at[sweep, q, me - home * G], (w // R, w % R, home)
        )

    def sweep_of(sweep, tile_a, tile_b, a_transposed):
        gather(sweep)
        acca[...] = jnp.zeros_like(acca)
        accb[...] = jnp.zeros_like(accb)

        def step_a(s, carry):
            if sweep == 0:
                v_tile(s).wait()
                masked(va, mv, s)
            lhs = xa[:, :, pl.ds(s, 1)].reshape(rows, vir)
            acca[...] += product(lhs, tile_a, s, a_transposed)
            each = -(-nch // tall)
            for e in range(each):
                t = s * each + e

                @pl.when(t < nch)
                def _():
                    pass_on(t)

            return carry

        lax.fori_loop(0, tall, step_a, 0)
        count = rows // C
        for k in range(1, C):
            begin = pl.multiple_of(((q + k) % C) * count, count)
            sa[k - 1] = acca[pl.ds(begin, count), :].astype(sa.dtype)
            exchange_a(sweep, k).start()
        lax.fori_loop(0, nch, settle, 0)

        def step_b(s, carry):
            if sweep == 0:
                w_tile(s).wait()
                masked(wa, mw, s)
            wl, r = s // wide, s % wide
            blocks = [xa[q * G + wl, r].reshape(tall * occ, vir)]
            for slot in range(C - 1):
                blocks.append(xb[slot, wl, r].reshape(tall * occ, vir))
            accb[...] += product(jnp.concatenate(blocks, axis=0), tile_b, s, not a_transposed)
            return carry

        lax.fori_loop(0, tall, step_b, 0)
        if sweep == 0:
            for device in [after, before, sibling] + [(z, row, (q + k) % C) for k in range(1, C)]:
                pl.semaphore_signal(ready, inc=1, device_id=device, device_id_type=MESH)
        sb[...] = accb[...].reshape(sb.shape).astype(sb.dtype)

        def send(k, carry):
            w, block, copy = exchange_b(sweep, k)
            local = jnp.logical_and(w == me, home == q)

            @pl.when(local)
            def _():
                rb[sweep, q, me - home * G] = sb[block]

            @pl.when(jnp.logical_not(local))
            def _():
                copy.start()

            return carry

        lax.fori_loop(0, W, send, 0)
        for k in range(1, C):
            exchange_a(sweep, k).wait()

        def arrive(n, carry):
            c, wl = n // G, n % G

            @pl.when(jnp.logical_or(c != q, q * G + wl != me))
            def _():
                piece = rb.at[sweep, c, wl]
                remote(piece, piece, eb_s.at[0], eb_r.at[sweep, c, wl], sibling).wait_recv()

            return carry

        lax.fori_loop(0, W, arrive, 0)

        def sent(k, carry):
            w, block, copy = exchange_b(sweep, k)

            @pl.when(jnp.logical_not(jnp.logical_and(w == me, home == q)))
            def _():
                copy.wait_send()

            return carry

        lax.fori_loop(0, W, sent, 0)

        def assemble(wl, carry):
            for r in range(wide):
                place_r = wl * wide + r
                for s in range(wide):
                    lanes = pl.ds(s * vir, vir)
                    begin = pl.multiple_of((q * tall + place_r) * occ, occ)
                    total = acca[pl.ds(begin, occ), lanes]
                    for slot in range(C - 1):
                        here = pl.ds(pl.multiple_of(place_r * occ, occ), occ)
                        total += ra[sweep, slot, here, lanes].astype(jnp.float32)
                    for c in range(C):
                        total += rb[sweep, c, wl, pl.ds(s * occ, occ), pl.ds(r * vir, vir)].astype(jnp.float32)
                    if sweep == 0:
                        total += drv[s, place_r].astype(jnp.float32)
                        value = total / (base[...] + shift_one[s, place_r])
                        out_one[s, place_r] = value
                        xa[me, s, place_r] = value.astype(xa.dtype)
                    else:
                        out_two[s, place_r] = total / (base[...] + shift_two[s, place_r])
            return carry

        lax.fori_loop(0, G, assemble, 0)
        if sweep == 0:
            pl.semaphore_wait(ready, C + 2)

    lax.fori_loop(0, tall, load, 0)
    sweep_of(0, va, wa, False)
    sweep_of(1, wa, va, True)


def body(
    amps, driver, ladder_operator, ladder_block_mask, cycle_op, cycle_mask, occ_i, occ_j, vir_a, vir_b,
):
    S, R, C = lax.axis_size("sec"), lax.axis_size("row"), lax.axis_size("col")
    W = S * R
    G = W // C
    nch = W // 2
    wide_index = lax.axis_index(("sec", "row"))
    col_index = lax.axis_index("col")
    occ, wide, tall, vir = amps.shape
    rows = W * wide * occ
    span = wide * vir
    x = jnp.transpose(amps, (1, 2, 0, 3))
    drv = jnp.transpose(driver, (2, 1, 0, 3))
    edge_v = ladder_operator.shape[1] // ladder_block_mask.shape[1]
    edge_w = cycle_op.shape[1] // cycle_mask.shape[1]
    mv = jnp.repeat(ladder_block_mask.astype(jnp.float32), edge_v, axis=1).reshape(tall, -1, span)
    mw = jnp.repeat(cycle_mask.astype(jnp.float32), edge_w, axis=1)
    mw = jnp.transpose(mw.reshape(cycle_mask.shape[0], tall, vir), (1, 0, 2))
    base = vir_b[None, :] - occ_i[:, None]
    shift_one = (
        lax.dynamic_slice_in_dim(vir_a, wide_index * wide, wide)[:, None]
        - lax.dynamic_slice_in_dim(occ_j, col_index * tall, tall)[None, :]
    )
    shift_two = (
        lax.dynamic_slice_in_dim(vir_a, col_index * tall, tall)[None, :]
        - lax.dynamic_slice_in_dim(occ_j, wide_index * wide, wide)[:, None]
    )
    vmem = pl.BlockSpec(memory_space=pltpu.VMEM)
    smem = pl.BlockSpec(memory_space=pltpu.SMEM)
    hbm = pl.BlockSpec(memory_space=pl.ANY)
    dma = pltpu.SemaphoreType.DMA
    half = jnp.bfloat16
    result = jax.ShapeDtypeStruct((wide, tall, occ, vir), jnp.float32)
    one, two = pl.pallas_call(
        functools.partial(kernel, (S, R, C)),
        out_shape=(result, result),
        in_specs=[hbm, vmem, hbm, hbm, vmem, vmem, vmem, smem, smem],
        out_specs=(vmem, vmem),
        scratch_shapes=[
            pltpu.VMEM((tall, vir, span), half),
            pltpu.VMEM((tall, span, vir), half),
            pltpu.VMEM((W, wide, tall, occ, vir), half),
            pltpu.VMEM((C - 1, G, wide, tall, occ, vir), half),
            pltpu.VMEM((rows, span), jnp.float32),
            pltpu.VMEM((rows, span), jnp.float32),
            pltpu.VMEM((C - 1, rows // C, span), half),
            pltpu.VMEM((W, wide * occ, span), half),
            pltpu.VMEM((2, C - 1, rows // C, span), half),
            pltpu.VMEM((2, C, G, wide * occ, span), half),
            dma((2, tall)),
            dma,
            dma((2, nch)),
            dma((2, nch)),
            dma((2, nch)),
            dma((2, nch)),
            dma((2, nch)),
            dma((C - 1, 2, nch)),
            dma((C - 1, 2, nch)),
            dma((C - 1, 2, nch)),
            dma((C - 1,)),
            dma((2, C - 1)),
            dma((W,)),
            dma((2, C, G)),
            pltpu.SemaphoreType.REGULAR,
        ],
        compiler_params=pltpu.CompilerParams(
            collective_id=0, has_side_effects=True, vmem_limit_bytes=63 * 1024 * 1024
        ),
    )(x, drv, ladder_operator, cycle_op, mv, mw, base, shift_one, shift_two)
    return jnp.transpose(one, (2, 1, 0, 3)), jnp.transpose(two, (2, 0, 1, 3))


def solution(mesh):
    placed = (
        P(None, ("sec", "row"), "col", None),
        P(None, "col", ("sec", "row"), None),
        P("col", ("sec", "row")),
        P("col", ("sec", "row")),
        P(("sec", "row"), "col"),
        P(("sec", "row"), "col"),
        P(),
        P(),
        P(),
        P(),
    )
    return jax.shard_map(
        body,
        mesh=mesh,
        in_specs=placed,
        out_specs=(P(None, "col", ("sec", "row"), None), P(None, ("sec", "row"), "col", None)),
        check_vma=False,
    )
```

time: 766 us -> 236 us (0.31); the launches traced: 753 us -> 235 us
  waiting for transfers between devices: 509 us -> 0 us
  Pallas kernels: 0 us -> 216 us
  local copies, waits for them, and re-layouts: 125 us -> 15 us
  matrix products: 76.7 us -> 0 us
  other arithmetic: 28 us -> 3.41 us
  between operations: 14.5 us -> 0.68 us
    reduce_scatter x4 -> x0, waiting for transfers between devices: 352 us -> none  [the longest x1 176 us: body(): lax.psum_scatter(ladder_part_two, ('sec', 'row'), scatter_dimension=1, ti...]
    pallas_call x0 -> x1, Pallas kernels: none -> 216 us  [body(): pl.pallas_call(functools.partial(kernel, (S, R, C)), out_shape=(result, r...]
    all_gather x4 -> x0, waiting for transfers between devices: 155 us -> none  [the longest x1 73.6 us: body(): piece = lax.all_gather(amp_rounded, ('sec', 'row'), axis=2, tiled=True)]
    dot_general x4 -> x0, matrix products: 76.7 us -> none  [the longest x2 44.6 us: product_transposed(): lax.dot_general(rows, tile, (((1,), (1,)), ((), ())), preferred_element_t...]
    dot_general x6 -> x0, local copies, waits for them, and re-layouts: 54.7 us -> none  [the longest x4 35.4 us: product_transposed(): lax.dot_general(rows, tile, (((1,), (1,)), ((), ())), preferred_element_t...]
    unnamed x17 -> x4, local copies, waits for them, and re-layouts: 42 us -> 10.1 us
    mul x2 -> x0, other arithmetic: 20.4 us -> none  [tile_masked(): shaped * mask[:, None, :, None].astype(tile.dtype)]
    reshape x3 -> x0, local copies, waits for them, and re-layouts: 13.2 us -> none  [the longest x2 6.95 us: body(): ladder_part = result.reshape(occupied, count, vir_wide, virtuals)]
  transfers between devices with their start and end apart: 8 -> 0, of which waited for: 5 -> 0; matrix products, arithmetic and copies ran while one was open for 23% -> 0% of each run, Pallas kernels for 0% -> 0%
where the time goes in v1:
time: 236 us; the launch traced here: 235 us
  Pallas kernels  216 us (92%)
  local copies, waits for them, and re-layouts  15 us (6%)
  other arithmetic  3.41 us (1%)
    pallas_call x1, Pallas kernels, body(): pl.pallas_call(functools.partial(kernel, (S, R, C)), out_shape=(result, r...  216 us
    unnamed x4, local copies, waits for them, and re-layouts  10.1 us

profile of v1, /device:TPU:15, one launch (start us, length us, event | category | flops | bytes accessed | tf_op | source)
XLA Modules:
  0.0 235.3 jit_solution(1348044241418945853)
XLA Ops:
  0.6 0.7 dynamic_slice.15
  1.4 0.7 dynamic_slice.12
  2.1 0.7 dynamic_slice.13
  2.8 0.7 dynamic_slice.14
  3.6 0.7 broadcast_subtract_fusion.1
  4.2 0.7 convert_element_type.6
  4.9 0.7 convert_element_type.7
  5.6 0.1 copy.19
  5.7 1.4 broadcast_subtract_fusion.base
  7.1 0.1 broadcast_in_dim.4
  7.2 0.8 reshape_reshape.6.mv
  8.0 0.1 broadcast_in_dim.5
  8.2 0.9 copy.28
  9.1 2.1 copy.27
  11.2 2.1 copy.26
  13.3 216.2 %shard_map.113 = (f32[2,16,16,512]{3,2,1,0:T(8,128)}, f32[2,16,16,512]{3,2,1,0:T(8,128)}) custom-call(bf16[2,16,16,512]{3,2,1,0:T(8,128)(2,1)} %bitcast.11, bf16[2,16,16,512]{3,2,1,0:T(8,128)(2,1)} %bitcast.12, bf16[8192,1024]{1,0:T(8,128)(2,1)} %v_hbm.1, bf16[1024,8192]{1,0:T(8,128)(2,1)} %w_hbm.1, f32[16,4,1024]{2,1,0:T(4,128)} %reshape_reshape.6.mv, ...), custom_call_target="tpu_custom_call" | custom-call | tf_op jit(solution)/shard_map/pallas_call | solution.py:350
  229.5 3.0 %copy.21 = f32[16,16,2,512]{3,2,1,0:T(2,128)} copy(f32[16,16,2,512]{3,0,1,2:T(8,128)} %bitcast.15) | data formatting | bytes 2097152
  232.5 2.8 %copy.22 = f32[16,2,16,512]{3,2,1,0:T(8,128)} copy(f32[16,2,16,512]{3,0,2,1:T(8,128)} %bitcast.14) | data formatting | bytes 2097152
  (1 shorter events, 0.0 us)

commit v2 on v1

--- a/solution.py
+++ b/solution.py
@@ -11,8 +11,8 @@
 
 
 def kernel(
-    sizes, x, drv, v_hbm, w_hbm, mv, mw, base, shift_one, shift_two, out_one, out_two,
-    va, wa, xa, xb, acca, accb, sa, sb, ra, rb,
+    sizes, x, drv, v_hbm, w_hbm, mask_v, mask_w, occ_i, occ_j, vir_a, vir_b, out_one, out_two,
+    va, wa, xa, xb, acca, accb, sa, sb, ra, rb, base,
     tile_sem, own_sem, ring_s, ring_r, sib_s, sib_r, y_s, y_r, yb_s, yb_r,
     ea_s, ea_r, eb_s, eb_r, ready,
 ):
@@ -21,9 +21,12 @@
     G = W // C
     nch = W // 2
     wide, tall, occ, vir = xa.shape[1:]
-    half = tall // 2
-    rows = accb.shape[0]
-    edge = v_hbm.shape[0] // (mv.shape[0] * mv.shape[1])
+    ways = 2 if wide % 2 == 0 else 1
+    half = wide // ways
+    near = nch // 2
+    block_rows = half * occ
+    edge_v = v_hbm.shape[0] // mask_v.shape[0]
+    edge_w = w_hbm.shape[0] // mask_w.shape[0]
     z, row, q = lax.axis_index("sec"), lax.axis_index("row"), lax.axis_index("col")
     me = z * R + row
     core = row % 2
@@ -36,9 +39,18 @@
         xo, zo = o // S, o % S
         return xo, zo + (xo % 2) * (S - 1 - 2 * zo)
 
-    def wide_of(o):
+    def wide_of(o, which=None):
         xo, zo = place(o)
-        return zo * R + 2 * xo + core
+        return zo * R + 2 * xo + (core if which is None else which)
+
+    def row_of(w, r):
+        zo, ro = w // R, w % R
+        xo = ro // 2
+        o = xo * S + zo + (xo % 2) * (S - 1 - 2 * zo)
+        h, rest = r // half, r % half
+        d = (p - o + nch) % nch if h == 0 else (o - p + nch) % nch
+        index = (((d // near) * ways + h) * near + d % near) * 2 + ro % 2
+        return pl.multiple_of(index * block_rows + rest * occ, occ)
 
     def device_at(o):
         xo, zo = place(o)
@@ -58,11 +70,11 @@
         )
 
     def ring(t, h):
-        piece = xa.at[wide_of(origin(t, h)), :, part(h)]
+        piece = xa.at[wide_of(origin(t, h)), part(h)]
         return remote(piece, piece, ring_s.at[h, t], ring_r.at[h, t], after if h == 0 else before)
 
     def sib(t, h):
-        piece = xa.at[wide_of(origin(t, h)), :, part(h)]
+        piece = xa.at[wide_of(origin(t, h)), part(h)]
         return remote(piece, piece, sib_s.at[h, t], sib_r.at[h, t], sibling)
 
     def cross(t, h):
@@ -70,13 +82,13 @@
         goal = w // G
         slot = (q - goal - 1 + C) % C
         return goal, remote(
-            xa.at[w, :, part(h)], xb.at[slot, w - goal * G, :, part(h)],
+            xa.at[w, part(h)], xb.at[slot, w - goal * G, part(h)],
             y_s.at[h, t], y_r.at[slot, h, t], (z, row, goal),
         )
 
     def cross_in(t, h, slot):
         w = wide_of(origin(t, h))
-        piece = xb.at[slot, w - (w // G) * G, :, part(h)]
+        piece = xb.at[slot, w - (w // G) * G, part(h)]
         return w // G, piece
 
     barrier = pltpu.get_barrier_semaphore()
@@ -112,20 +124,72 @@
     own.wait()
     pl.semaphore_wait(barrier, W * C - 1)
 
-    def masked(tile, mask, s):
-        strips = mask.shape[1]
+    def cover(tile, s, rows, lanes, keep):
+        keep = jnp.full((rows.size, lanes.size), keep.astype(jnp.float32)).astype(tile.dtype)
+        tile[s, rows, lanes] = tile[s, rows, lanes] * keep
+
+    def mask_tiles(s):
+        strips, across = va.shape[1] // edge_v, va.shape[2] // edge_v
+        v_tile(s).wait()
         for b in range(strips):
-            span = pl.ds(b * edge, edge)
-            keep = jnp.broadcast_to(mask[s, pl.ds(b, 1), :], (edge, tile.shape[2])).astype(tile.dtype)
-            tile[s, span, :] = tile[s, span, :] * keep
+            for c in range(across):
+                cover(va, s, pl.ds(b * edge_v, edge_v), pl.ds(c * edge_v, edge_v), mask_v[s * strips + b, c])
+        strips, across = wa.shape[1] // edge_w, wa.shape[2] // edge_w
+        w_tile(s).wait()
+        for b in range(strips):
+            for c in range(across):
+                cover(wa, s, pl.ds(b * edge_w, edge_w), pl.ds(c * edge_w, edge_w), mask_w[b, s * across + c])
 
     def product(lhs, tile, s, transposed):
         dims = (((1,), (1 if transposed else 0,)), ((), ()))
         return lax.dot_general(lhs, tile[s], dims, preferred_element_type=jnp.float32)
 
-    def gather(sweep):
+    def step_a(far, tile, s, transposed):
+        blocks = []
+        for h in range(ways):
+            for d in range(near):
+                o = origin(far * near + d, h)
+                for which in range(2):
+                    piece = xa[wide_of(o, which), pl.ds(h * half, half), pl.ds(s, 1)]
+                    blocks.append(piece.reshape(block_rows, vir))
+        count = len(blocks) * block_rows
+        span = pl.ds(far * count, count)
+        acca[span, :] += product(jnp.concatenate(blocks, axis=0), tile, s, transposed)
+
+    def unit_b(source, wl, h, slot, tile, transposed):
+        for rest in range(half):
+            r = h * half + rest
+            lhs = source[r].reshape(tall * occ, vir)
+            accb[slot] += product(lhs, tile, wl * wide + r, transposed)
+
+    def own_units(t, tile, transposed):
+        for h in range(ways):
+            w = wide_of(origin(t, h), 0)
+
+            @pl.when(w // G == q)
+            def _():
+                for which in range(2):
+                    unit_b(xa.at[w + which], w + which - q * G, h, 0, tile, transposed)
+
+    def cross_units(t, tile, transposed):
+        for h in range(ways):
+            w = wide_of(origin(t, h), 0)
+
+            @pl.when(w // G == q)
+            def _():
+                for slot in range(C - 1):
+                    wl = w + core - q * G
+                    unit_b(xb.at[slot, wl], wl, h, 1 + slot, tile, transposed)
+                    wl = w + 1 - core - q * G
+                    piece = xb.at[slot, wl, part(h)]
+                    remote(piece, piece, yb_s.at[slot, h, t], yb_r.at[slot, h, t], sibling).wait_recv()
+                    unit_b(xb.at[slot, wl], wl, h, 1 + slot, tile, transposed)
+
+    def gather(sweep, tile_a, tile_b, a_transposed):
+        each = -(-tall // near)
+
         def slot_step(t, carry):
-            for h in range(2):
+            for h in range(ways):
                 @pl.when(t >= 1)
                 def _():
                     ring(t - 1, h).wait_recv()
@@ -141,19 +205,48 @@
                 def _():
                     copy.start()
 
+            @pl.when(t >= 1)
+            def _():
+                for h in range(ways):
+                    sib(t - 1, h).wait_recv()
+
+            def work(n, carry):
+                s = (t % near) * each + n
+
+                @pl.when(s < tall)
+                def _():
+                    if sweep == 0:
+                        @pl.when(t < near)
+                        def _():
+                            mask_tiles(s)
+
+                    @pl.when(t >= near)
+                    def _():
+                        step_a(0, tile_a, s, a_transposed)
+
+                return carry
+
+            lax.fori_loop(0, each, work, 0)
+
+            def pair(n, carry):
+                d = 2 * (t - near) + n
+
+                @pl.when(jnp.logical_and(d >= 0, d < t))
+                def _():
+                    own_units(d, tile_b, not a_transposed)
+
+                return carry
+
+            lax.fori_loop(0, 2, pair, 0)
             return carry
 
         lax.fori_loop(0, nch, slot_step, 0)
-
-        def landed(t, carry):
-            for h in range(2):
-                sib(t, h).wait_recv()
-            return carry
-
-        lax.fori_loop(0, nch, landed, 0)
+        for h in range(ways):
+            sib(nch - 1, h).wait_recv()
+        own_units(nch - 1, tile_b, not a_transposed)
 
     def pass_on(t):
-        for h in range(2):
+        for h in range(ways):
             for slot in range(C - 1):
                 mine, piece = cross_in(t, h, slot)
 
@@ -163,13 +256,13 @@
                     remote(piece, piece, yb_s.at[slot, h, t], yb_r.at[slot, h, t], sibling).start()
 
     def settle(t, carry):
-        for h in range(2):
+        for h in range(ways):
             for slot in range(C - 1):
                 mine, piece = cross_in(t, h, slot)
 
                 @pl.when(mine == q)
                 def _():
-                    remote(piece, piece, yb_s.at[slot, h, t], yb_r.at[slot, h, t], sibling).wait()
+                    remote(piece, piece, yb_s.at[slot, h, t], yb_r.at[slot, h, t], sibling).wait_send()
 
             @pl.when(t < nch - 1)
             def _():
@@ -197,46 +290,38 @@
         )
 
     def sweep_of(sweep, tile_a, tile_b, a_transposed):
-        gather(sweep)
         acca[...] = jnp.zeros_like(acca)
         accb[...] = jnp.zeros_like(accb)
-
-        def step_a(s, carry):
-            if sweep == 0:
-                v_tile(s).wait()
-                masked(va, mv, s)
-            lhs = xa[:, :, pl.ds(s, 1)].reshape(rows, vir)
-            acca[...] += product(lhs, tile_a, s, a_transposed)
-            each = -(-nch // tall)
-            for e in range(each):
-                t = s * each + e
-
-                @pl.when(t < nch)
-                def _():
-                    pass_on(t)
-
-            return carry
-
-        lax.fori_loop(0, tall, step_a, 0)
-        count = rows // C
+        gather(sweep, tile_a, tile_b, a_transposed)
+
+        def rest_a(s, carry):
+            step_a(1, tile_a, s, a_transposed)
+            return carry
+
+        lax.fori_loop(0, tall, rest_a, 0)
+
+        def arrivals(t, carry):
+            pass_on(t)
+
+            @pl.when(t >= 1)
+            def _():
+                cross_units(t - 1, tile_b, not a_transposed)
+
+            return carry
+
+        lax.fori_loop(0, nch, arrivals, 0)
         for k in range(1, C):
-            begin = pl.multiple_of(((q + k) % C) * count, count)
-            sa[k - 1] = acca[pl.ds(begin, count), :].astype(sa.dtype)
+            def fill(wl, carry):
+                for r in range(wide):
+                    here = pl.ds(pl.multiple_of((wl * wide + r) * occ, occ), occ)
+                    there = pl.ds(row_of(((q + k) % C) * G + wl, r), occ)
+                    sa[k - 1, here, :] = acca[there, :].astype(sa.dtype)
+                return carry
+
+            lax.fori_loop(0, G, fill, 0)
             exchange_a(sweep, k).start()
+        cross_units(nch - 1, tile_b, not a_transposed)
         lax.fori_loop(0, nch, settle, 0)
-
-        def step_b(s, carry):
-            if sweep == 0:
-                w_tile(s).wait()
-                masked(wa, mw, s)
-            wl, r = s // wide, s % wide
-            blocks = [xa[q * G + wl, r].reshape(tall * occ, vir)]
-            for slot in range(C - 1):
-                blocks.append(xb[slot, wl, r].reshape(tall * occ, vir))
-            accb[...] += product(jnp.concatenate(blocks, axis=0), tile_b, s, not a_transposed)
-            return carry
-
-        lax.fori_loop(0, tall, step_b, 0)
         if sweep == 0:
             for device in [after, before, sibling] + [(z, row, (q + k) % C) for k in range(1, C)]:
                 pl.semaphore_signal(ready, inc=1, device_id=device, device_id_type=MESH)
@@ -288,8 +373,7 @@
                 place_r = wl * wide + r
                 for s in range(wide):
                     lanes = pl.ds(s * vir, vir)
-                    begin = pl.multiple_of((q * tall + place_r) * occ, occ)
-                    total = acca[pl.ds(begin, occ), lanes]
+                    total = acca[pl.ds(row_of(q * G + wl, r), occ), lanes]
                     for slot in range(C - 1):
                         here = pl.ds(pl.multiple_of(place_r * occ, occ), occ)
                         total += ra[sweep, slot, here, lanes].astype(jnp.float32)
@@ -297,11 +381,11 @@
                         total += rb[sweep, c, wl, pl.ds(s * occ, occ), pl.ds(r * vir, vir)].astype(jnp.float32)
                     if sweep == 0:
                         total += drv[s, place_r].astype(jnp.float32)
-                        value = total / (base[...] + shift_one[s, place_r])
+                        value = total / (base[...] + (vir_a[me * wide + s] - occ_j[q * tall + place_r]))
                         out_one[s, place_r] = value
                         xa[me, s, place_r] = value.astype(xa.dtype)
                     else:
-                        out_two[s, place_r] = total / (base[...] + shift_two[s, place_r])
+                        out_two[s, place_r] = total / (base[...] + (vir_a[q * tall + place_r] - occ_j[me * wide + s]))
             return carry
 
         lax.fori_loop(0, G, assemble, 0)
@@ -309,6 +393,8 @@
             pl.semaphore_wait(ready, C + 2)
 
     lax.fori_loop(0, tall, load, 0)
+    for i in range(occ):
+        base[pl.ds(i, 1), :] = vir_b[...] - occ_i[i]
     sweep_of(0, va, wa, False)
     sweep_of(1, wa, va, True)
 
@@ -320,27 +406,11 @@
     W = S * R
     G = W // C
     nch = W // 2
-    wide_index = lax.axis_index(("sec", "row"))
-    col_index = lax.axis_index("col")
     occ, wide, tall, vir = amps.shape
     rows = W * wide * occ
     span = wide * vir
     x = jnp.transpose(amps, (1, 2, 0, 3))
     drv = jnp.transpose(driver, (2, 1, 0, 3))
-    edge_v = ladder_operator.shape[1] // ladder_block_mask.shape[1]
-    edge_w = cycle_op.shape[1] // cycle_mask.shape[1]
-    mv = jnp.repeat(ladder_block_mask.astype(jnp.float32), edge_v, axis=1).reshape(tall, -1, span)
-    mw = jnp.repeat(cycle_mask.astype(jnp.float32), edge_w, axis=1)
-    mw = jnp.transpose(mw.reshape(cycle_mask.shape[0], tall, vir), (1, 0, 2))
-    base = vir_b[None, :] - occ_i[:, None]
-    shift_one = (
-        lax.dynamic_slice_in_dim(vir_a, wide_index * wide, wide)[:, None]
-        - lax.dynamic_slice_in_dim(occ_j, col_index * tall, tall)[None, :]
-    )
-    shift_two = (
-        lax.dynamic_slice_in_dim(vir_a, col_index * tall, tall)[None, :]
-        - lax.dynamic_slice_in_dim(occ_j, wide_index * wide, wide)[:, None]
-    )
     vmem = pl.BlockSpec(memory_space=pltpu.VMEM)
     smem = pl.BlockSpec(memory_space=pltpu.SMEM)
     hbm = pl.BlockSpec(memory_space=pl.ANY)
@@ -350,7 +420,7 @@
     one, two = pl.pallas_call(
         functools.partial(kernel, (S, R, C)),
         out_shape=(result, result),
-        in_specs=[hbm, vmem, hbm, hbm, vmem, vmem, vmem, smem, smem],
+        in_specs=[hbm, vmem, hbm, hbm, smem, smem, smem, smem, smem, vmem],
         out_specs=(vmem, vmem),
         scratch_shapes=[
             pltpu.VMEM((tall, vir, span), half),
@@ -358,11 +428,12 @@
             pltpu.VMEM((W, wide, tall, occ, vir), half),
             pltpu.VMEM((C - 1, G, wide, tall, occ, vir), half),
             pltpu.VMEM((rows, span), jnp.float32),
-            pltpu.VMEM((rows, span), jnp.float32),
+            pltpu.VMEM((C, tall * occ, span), jnp.float32),
             pltpu.VMEM((C - 1, rows // C, span), half),
             pltpu.VMEM((W, wide * occ, span), half),
             pltpu.VMEM((2, C - 1, rows // C, span), half),
             pltpu.VMEM((2, C, G, wide * occ, span), half),
+            pltpu.VMEM((occ, vir), jnp.float32),
             dma((2, tall)),
             dma,
             dma((2, nch)),
@@ -382,7 +453,7 @@
         compiler_params=pltpu.CompilerParams(
             collective_id=0, has_side_effects=True, vmem_limit_bytes=63 * 1024 * 1024
         ),
-    )(x, drv, ladder_operator, cycle_op, mv, mw, base, shift_one, shift_two)
+    )(x, drv, ladder_operator, cycle_op, ladder_block_mask, cycle_mask, occ_i, occ_j, vir_a, vir_b[None])
     return jnp.transpose(one, (2, 1, 0, 3)), jnp.transpose(two, (2, 0, 1, 3))
 
 

time: 236 us -> 217 us (0.919)
  Pallas kernels: 216 us -> 202 us
  local copies, waits for them, and re-layouts: 15 us -> 11.4 us
  other arithmetic: 3.41 us -> 0 us
    pallas_call x1, Pallas kernels: 216 us -> 202 us  [body(): pl.pallas_call(functools.partial(kernel, (S, R, C)), out_shape=(result, r...]
    dynamic_slice x4 -> x0, local copies, waits for them, and re-layouts: 2.91 us -> none  [the longest x1 0.73 us: body(): lax.dynamic_slice_in_dim(occ_j, wide_index * wide, wide)[:, None]]
    unnamed x4 -> x5, local copies, waits for them, and re-layouts: 10.1 us -> 11.4 us
where the time goes in v2:
time: 217 us; the launch traced here: 215 us
  Pallas kernels  202 us (93%)
  local copies, waits for them, and re-layouts  11.4 us (5%)
    pallas_call x1, Pallas kernels, body(): pl.pallas_call(functools.partial(kernel, (S, R, C)), out_shape=(result, r...  202 us
    unnamed x5, local copies, waits for them, and re-layouts  11.4 us

profile of v2, /device:TPU:15, one launch (start us, length us, event | category | flops | bytes accessed | tf_op | source)
XLA Modules:
  0.0 214.5 jit_solution(17774231695143122701)
XLA Ops:
  0.6 1.4 copy.14.mask_v
  2.0 2.1 copy.20
  4.1 2.1 copy.19
  6.3 202.4 %shard_map.113 = (f32[2,16,16,512]{3,2,1,0:T(8,128)}, f32[2,16,16,512]{3,2,1,0:T(8,128)}) custom-call(bf16[2,16,16,512]{3,2,1,0:T(8,128)(2,1)} %bitcast.9, bf16[2,16,16,512]{3,2,1,0:T(8,128)(2,1)} %bitcast.10, bf16[8192,1024]{1,0:T(8,128)(2,1)} %v_hbm.1, bf16[1024,8192]{1,0:T(8,128)(2,1)} %w_hbm.1, s32[64,8]{1,0:T(8,128)} %copy.14.mask_v, s32[8,64]{1,0:T(8,128)} %mask_w.1, ...), custom_call_target="tpu_custom_call" | custom-call | tf_op jit(solution)/shard_map/pallas_call | solution.py:420
  208.7 3.0 %copy.15 = f32[16,16,2,512]{3,2,1,0:T(2,128)} copy(f32[16,16,2,512]{3,0,1,2:T(8,128)} %bitcast.12) | data formatting | bytes 2097152
  211.7 2.8 %copy.16 = f32[16,2,16,512]{3,2,1,0:T(8,128)} copy(f32[16,2,16,512]{3,0,2,1:T(8,128)} %bitcast.11) | data formatting | bytes 2097152

commit v3 on v2

--- a/solution.py
+++ b/solution.py
@@ -33,7 +33,6 @@
     xchip = row // 2
     p = xchip * S + z + (xchip % 2) * (S - 1 - 2 * z)
     sibling = (z, row + 1 - 2 * core, q)
-    home = me // G
 
     def place(o):
         xo, zo = o // S, o % S
@@ -277,17 +276,29 @@
 
         return carry
 
-    def exchange_a(sweep, k):
+    def exchange_a(sweep, k, wl):
         return remote(
-            sa.at[k - 1], ra.at[sweep, C - 1 - k], ea_s.at[k - 1], ea_r.at[sweep, C - 1 - k], (z, row, (q + k) % C)
+            sa.at[k - 1, wl], ra.at[sweep, C - 1 - k, wl],
+            ea_s.at[k - 1, wl], ea_r.at[sweep, C - 1 - k, wl], (z, row, (q + k) % C),
         )
 
     def exchange_b(sweep, k):
         w = (me + k) % W
         block = ((w // G - q + C) % C) * G + w % G
-        return w, block, remote(
-            sb.at[block], rb.at[sweep, q, me - home * G], eb_s.at[k], eb_r.at[sweep, q, me - home * G], (w // R, w % R, home)
+        return block, remote(
+            sb.at[block], rb.at[sweep, me], eb_s.at[k], eb_r.at[sweep, me], (w // R, w % R, q)
         )
+
+    def arrive(sweep, w):
+        @pl.when(w != me)
+        def _():
+            piece = rb.at[sweep, w]
+            remote(piece, piece, eb_s.at[0], eb_r.at[sweep, w], sibling).wait_recv()
+
+    def plane_sum(sweep, w, r, s):
+        lanes = pl.ds(s * vir, vir)
+        both = acca[pl.ds(row_of(w, r), occ), lanes]
+        return both + rb[sweep, w, pl.ds(s * occ, occ), pl.ds(r * vir, vir)].astype(jnp.float32)
 
     def sweep_of(sweep, tile_a, tile_b, a_transposed):
         acca[...] = jnp.zeros_like(acca)
@@ -310,16 +321,6 @@
             return carry
 
         lax.fori_loop(0, nch, arrivals, 0)
-        for k in range(1, C):
-            def fill(wl, carry):
-                for r in range(wide):
-                    here = pl.ds(pl.multiple_of((wl * wide + r) * occ, occ), occ)
-                    there = pl.ds(row_of(((q + k) % C) * G + wl, r), occ)
-                    sa[k - 1, here, :] = acca[there, :].astype(sa.dtype)
-                return carry
-
-            lax.fori_loop(0, G, fill, 0)
-            exchange_a(sweep, k).start()
         cross_units(nch - 1, tile_b, not a_transposed)
         lax.fori_loop(0, nch, settle, 0)
         if sweep == 0:
@@ -327,58 +328,35 @@
                 pl.semaphore_signal(ready, inc=1, device_id=device, device_id_type=MESH)
         sb[...] = accb[...].reshape(sb.shape).astype(sb.dtype)
 
+        rb[sweep, me] = sb[me % G + ((me // G - q + C) % C) * G]
+
         def send(k, carry):
-            w, block, copy = exchange_b(sweep, k)
-            local = jnp.logical_and(w == me, home == q)
-
-            @pl.when(local)
-            def _():
-                rb[sweep, q, me - home * G] = sb[block]
-
-            @pl.when(jnp.logical_not(local))
-            def _():
-                copy.start()
-
-            return carry
-
-        lax.fori_loop(0, W, send, 0)
+            exchange_b(sweep, k)[1].start()
+            return carry
+
+        lax.fori_loop(1, W, send, 0)
         for k in range(1, C):
-            exchange_a(sweep, k).wait()
-
-        def arrive(n, carry):
-            c, wl = n // G, n % G
-
-            @pl.when(jnp.logical_or(c != q, q * G + wl != me))
-            def _():
-                piece = rb.at[sweep, c, wl]
-                remote(piece, piece, eb_s.at[0], eb_r.at[sweep, c, wl], sibling).wait_recv()
-
-            return carry
-
-        lax.fori_loop(0, W, arrive, 0)
-
-        def sent(k, carry):
-            w, block, copy = exchange_b(sweep, k)
-
-            @pl.when(jnp.logical_not(jnp.logical_and(w == me, home == q)))
-            def _():
-                copy.wait_send()
-
-            return carry
-
-        lax.fori_loop(0, W, sent, 0)
+            def fill(wl, carry):
+                w = ((q + k) % C) * G + wl
+                arrive(sweep, w)
+                for r in range(wide):
+                    for s in range(wide):
+                        sa[k - 1, wl, pl.ds(r * occ, occ), pl.ds(s * vir, vir)] = plane_sum(sweep, w, r, s).astype(sa.dtype)
+                exchange_a(sweep, k, wl).start()
+                return carry
+
+            lax.fori_loop(0, G, fill, 0)
 
         def assemble(wl, carry):
+            arrive(sweep, q * G + wl)
+            for k in range(1, C):
+                exchange_a(sweep, k, wl).wait()
             for r in range(wide):
                 place_r = wl * wide + r
                 for s in range(wide):
-                    lanes = pl.ds(s * vir, vir)
-                    total = acca[pl.ds(row_of(q * G + wl, r), occ), lanes]
+                    total = plane_sum(sweep, q * G + wl, r, s)
                     for slot in range(C - 1):
-                        here = pl.ds(pl.multiple_of(place_r * occ, occ), occ)
-                        total += ra[sweep, slot, here, lanes].astype(jnp.float32)
-                    for c in range(C):
-                        total += rb[sweep, c, wl, pl.ds(s * occ, occ), pl.ds(r * vir, vir)].astype(jnp.float32)
+                        total += ra[sweep, slot, wl, pl.ds(r * occ, occ), pl.ds(s * vir, vir)].astype(jnp.float32)
                     if sweep == 0:
                         total += drv[s, place_r].astype(jnp.float32)
                         value = total / (base[...] + (vir_a[me * wide + s] - occ_j[q * tall + place_r]))
@@ -389,6 +367,12 @@
             return carry
 
         lax.fori_loop(0, G, assemble, 0)
+
+        def sent(k, carry):
+            exchange_b(sweep, k)[1].wait_send()
+            return carry
+
+        lax.fori_loop(1, W, sent, 0)
         if sweep == 0:
             pl.semaphore_wait(ready, C + 2)
 
@@ -429,10 +413,10 @@
             pltpu.VMEM((C - 1, G, wide, tall, occ, vir), half),
             pltpu.VMEM((rows, span), jnp.float32),
             pltpu.VMEM((C, tall * occ, span), jnp.float32),
-            pltpu.VMEM((C - 1, rows // C, span), half),
+            pltpu.VMEM((C - 1, G, wide * occ, span), half),
             pltpu.VMEM((W, wide * occ, span), half),
-            pltpu.VMEM((2, C - 1, rows // C, span), half),
-            pltpu.VMEM((2, C, G, wide * occ, span), half),
+            pltpu.VMEM((2, C - 1, G, wide * occ, span), half),
+            pltpu.VMEM((2, W, wide * occ, span), half),
             pltpu.VMEM((occ, vir), jnp.float32),
             dma((2, tall)),
             dma,
@@ -444,10 +428,10 @@
             dma((C - 1, 2, nch)),
             dma((C - 1, 2, nch)),
             dma((C - 1, 2, nch)),
-            dma((C - 1,)),
-            dma((2, C - 1)),
+            dma((C - 1, G)),
+            dma((2, C - 1, G)),
             dma((W,)),
-            dma((2, C, G)),
+            dma((2, W)),
             pltpu.SemaphoreType.REGULAR,
         ],
         compiler_params=pltpu.CompilerParams(

time: 217 us -> 228 us (1.051)
  Pallas kernels: 202 us -> 215 us
    pallas_call x1, Pallas kernels: 202 us -> 215 us  [body(): pl.pallas_call(functools.partial(kernel, (S, R, C)), out_shape=(result, r...]
where the time goes in v3:
time: 228 us; the launch traced here: 227 us
  Pallas kernels  215 us (94%)
  local copies, waits for them, and re-layouts  11.4 us (5%)
    pallas_call x1, Pallas kernels, body(): pl.pallas_call(functools.partial(kernel, (S, R, C)), out_shape=(result, r...  215 us
    unnamed x5, local copies, waits for them, and re-layouts  11.4 us

profile of v3, /device:TPU:15, one launch (start us, length us, event | category | flops | bytes accessed | tf_op | source)
XLA Modules:
  0.0 227.2 jit_solution(16393440438081943983)
XLA Ops:
  0.6 1.4 copy.14.mask_v
  2.0 2.1 copy.20
  4.1 2.1 copy.19
  6.3 215.1 %shard_map.113 = (f32[2,16,16,512]{3,2,1,0:T(8,128)}, f32[2,16,16,512]{3,2,1,0:T(8,128)}) custom-call(bf16[2,16,16,512]{3,2,1,0:T(8,128)(2,1)} %bitcast.9, bf16[2,16,16,512]{3,2,1,0:T(8,128)(2,1)} %bitcast.10, bf16[8192,1024]{1,0:T(8,128)(2,1)} %v_hbm.1, bf16[1024,8192]{1,0:T(8,128)(2,1)} %w_hbm.1, s32[64,8]{1,0:T(8,128)} %copy.14.mask_v, s32[8,64]{1,0:T(8,128)} %mask_w.1, ...), custom_call_target="tpu_custom_call" | custom-call | tf_op jit(solution)/shard_map/pallas_call | solution.py:404
  221.4 3.0 %copy.15 = f32[16,16,2,512]{3,2,1,0:T(2,128)} copy(f32[16,16,2,512]{3,0,1,2:T(8,128)} %bitcast.12) | data formatting | bytes 2097152
  224.4 2.8 %copy.16 = f32[16,2,16,512]{3,2,1,0:T(8,128)} copy(f32[16,2,16,512]{3,0,2,1:T(8,128)} %bitcast.11) | data formatting | bytes 2097152

commit v4 on v2

--- a/solution.py
+++ b/solution.py
@@ -229,7 +229,7 @@
             lax.fori_loop(0, each, work, 0)
 
             def pair(n, carry):
-                d = 2 * (t - near) + n
+                d = 2 * (t - near) + n if sweep == 0 else t - 1
 
                 @pl.when(jnp.logical_and(d >= 0, d < t))
                 def _():
@@ -237,7 +237,7 @@
 
                 return carry
 
-            lax.fori_loop(0, 2, pair, 0)
+            lax.fori_loop(0, 2 if sweep == 0 else 1, pair, 0)
             return carry
 
         lax.fori_loop(0, nch, slot_step, 0)
@@ -294,13 +294,19 @@
         accb[...] = jnp.zeros_like(accb)
         gather(sweep, tile_a, tile_b, a_transposed)
 
-        def rest_a(s, carry):
-            step_a(1, tile_a, s, a_transposed)
-            return carry
-
-        lax.fori_loop(0, tall, rest_a, 0)
+        each = -(-tall // nch)
 
         def arrivals(t, carry):
+            def rest_a(n, carry):
+                s = t * each + n
+
+                @pl.when(s < tall)
+                def _():
+                    step_a(1, tile_a, s, a_transposed)
+
+                return carry
+
+            lax.fori_loop(0, each, rest_a, 0)
             pass_on(t)
 
             @pl.when(t >= 1)

time: 217 us -> 213 us (0.982)
  no operation moved by 1% of the time
where the time goes in v4:
time: 213 us; the launch traced here: 212 us
  Pallas kernels  200 us (94%)
  local copies, waits for them, and re-layouts  11.4 us (5%)
    pallas_call x1, Pallas kernels, body(): pl.pallas_call(functools.partial(kernel, (S, R, C)), out_shape=(result, r...  200 us
    unnamed x5, local copies, waits for them, and re-layouts  11.4 us

profile of v4, /device:TPU:15, one launch (start us, length us, event | category | flops | bytes accessed | tf_op | source)
XLA Modules:
  0.0 212.4 jit_solution(2362208311249557709)
XLA Ops:
  0.6 1.4 copy.14.mask_v
  2.0 2.1 %copy.20 = bf16[16,2,16,512]{3,0,2,1:T(8,128)(2,1)} copy(bf16[16,2,16,512]{3,2,1,0:T(8,128)(2,1)} %param.10) | data formatting | bytes 1048576 | tf_op args[0]
  4.1 2.1 %copy.19 = bf16[16,16,2,512]{3,0,1,2:T(8,128)(2,1)} copy(bf16[16,16,2,512]{3,2,1,0:T(2,128)(2,1)} %param.11) | data formatting | bytes 1048576 | tf_op args[1]
  6.3 200.3 %shard_map.113 = (f32[2,16,16,512]{3,2,1,0:T(8,128)}, f32[2,16,16,512]{3,2,1,0:T(8,128)}) custom-call(bf16[2,16,16,512]{3,2,1,0:T(8,128)(2,1)} %bitcast.9, bf16[2,16,16,512]{3,2,1,0:T(8,128)(2,1)} %bitcast.10, bf16[8192,1024]{1,0:T(8,128)(2,1)} %v_hbm.1, bf16[1024,8192]{1,0:T(8,128)(2,1)} %w_hbm.1, s32[64,8]{1,0:T(8,128)} %copy.14.mask_v, s32[8,64]{1,0:T(8,128)} %mask_w.1, ...), custom_call_target="tpu_custom_call" | custom-call | tf_op jit(solution)/shard_map/pallas_call | solution.py:426
  206.6 3.0 %copy.15 = f32[16,16,2,512]{3,2,1,0:T(2,128)} copy(f32[16,16,2,512]{3,0,1,2:T(8,128)} %bitcast.12) | data formatting | bytes 2097152
  209.6 2.8 %copy.16 = f32[16,2,16,512]{3,2,1,0:T(8,128)} copy(f32[16,2,16,512]{3,0,2,1:T(8,128)} %bitcast.11) | data formatting | bytes 2097152
